TPU v7x, 32 devices: a whole 2x2x4 slice. The times are simulated.
32 devices in a mesh: dp: 4 (over y, x), fsdp: 8 (over z, core).
Axes of the slice: x: 2, y: 2, z: 4, core: 2. Of those that a mesh axis runs over, the one named last changes fastest.
Arguments:
- stream_in: bfloat16 [65536, 512], P(('dp', 'fsdp')), may hold values from -6 to 6
- dual_in: float32 [65536, 512], P(('dp', 'fsdp')), may hold values from -6 to 6
- segment_ids: int32 [64, 1024], P(('dp', 'fsdp')), may hold values from 0 to 8, as said below
- qkv_weight: float32 [512, 1536], P(('dp', 'fsdp')), may hold values from -0.25 to 0.25
- proj_weight: float32 [512, 512], P(('dp', 'fsdp')), may hold values from -1 to 1
- up_weight: float32 [512, 2048], P(('dp', 'fsdp')), may hold values from -0.25 to 0.25
- down_weight: float32 [2048, 512], P(('dp', 'fsdp')), may hold values from -0.1875 to 0.1875
- vectors: float32 [6144], P(('dp', 'fsdp')), may hold values from -1.2 to 2.2
- qkv_first: float32 [512, 1536], P(('dp', 'fsdp')), may hold values from -768 to 768
- proj_first: float32 [512, 512], P(('dp', 'fsdp')), may hold values from -320 to 320
- up_first: float32 [512, 2048], P(('dp', 'fsdp')), may hold values from -640 to 640
- down_first: float32 [2048, 512], P(('dp', 'fsdp')), may hold values from -1280 to 1280
- vec_first: float32 [6144], P(('dp', 'fsdp')), may hold values from -1024 to 1024
- qkv_second: float32 [512, 1536], P(('dp', 'fsdp')), may hold values from 16384 to 65536
- proj_second: float32 [512, 512], P(('dp', 'fsdp')), may hold values from 2621.44 to 10485.76
- up_second: float32 [512, 2048], P(('dp', 'fsdp')), may hold values from 10485.76 to 41943.04
- down_second: float32 [2048, 512], P(('dp', 'fsdp')), may hold values from 41943.04 to 167772.16
- vec_second: float32 [6144], P(('dp', 'fsdp')), may hold values from 6553.6 to 7864320
- cot_stream: bfloat16 [65536, 512], P(('dp', 'fsdp')), may hold values from -6 to 6
- cot_dual: bfloat16 [65536, 512], P(('dp', 'fsdp')), may hold values from -6 to 6
Outputs:
- stream_out: bfloat16 [65536, 512], P(('dp', 'fsdp'))
- dual_out: float32 [65536, 512], P(('dp', 'fsdp'))
- stream_grad: float32 [65536, 512], P(('dp', 'fsdp'))
- root_means: float32 [3], replicated
- qkv_grad: float32 [512, 1536], P(('dp', 'fsdp'))
- proj_grad: float32 [512, 512], P(('dp', 'fsdp'))
- up_grad: float32 [512, 2048], P(('dp', 'fsdp'))
- down_grad: float32 [2048, 512], P(('dp', 'fsdp'))
- vec_grad: float32 [6144], P(('dp', 'fsdp'))
- qkv_renewed: float32 [512, 1536], P(('dp', 'fsdp'))
- proj_renewed: float32 [512, 512], P(('dp', 'fsdp'))
- up_renewed: float32 [512, 2048], P(('dp', 'fsdp'))
- down_renewed: float32 [2048, 512], P(('dp', 'fsdp'))
- vec_renewed: float32 [6144], P(('dp', 'fsdp'))
- qkv_updated: float32 [512, 1536], P(('dp', 'fsdp'))
- proj_updated: float32 [512, 512], P(('dp', 'fsdp'))
- up_updated: float32 [512, 2048], P(('dp', 'fsdp'))
- down_updated: float32 [2048, 512], P(('dp', 'fsdp'))
- vec_updated: float32 [6144], P(('dp', 'fsdp'))
Inputs may be any that keep to these rules, and one draw needn't show every extreme that they name: `segment_ids`: in each row the nonzero ids start at 1 and never fall; padding (id 0) fills the row's tail; at least 256 positions of every row are nonzero; ids are at most min(8, 256), documents beyond that sharing the last number.
All inputs are finite; a program needn't handle non-finite values.
Results may differ from a plain program's by a relative error of at most 0.013.
The roundings to bfloat16 on the way count: a program that leaves them out, or rounds other values in their place, can miss the bound.
Values may be sent and summed in bfloat16 or wider, within the bound.
A program may use at most 256 MiB of HBM per device.

v0:
```python
import jax
import jax.numpy as jnp
from jax import lax
from jax.sharding import PartitionSpec as P

HEAD = 64
STEP = 10


NORM_EPS = 1e-05
BETA_FIRST = 0.5
BETA_SECOND = 0.5
ADAM_EPS = 1e-08


def normalize(summed, gain_vec, shift_vec):
    row_mean = jnp.mean(summed, axis=-1, keepdims=True)
    centred = summed - row_mean
    spread = jnp.mean(centred * centred, axis=-1, keepdims=True)
    return centred * lax.rsqrt(spread + NORM_EPS) * gain_vec + shift_vec


def smooth(values):
    return jax.nn.gelu(values, approximate=True)


def adam_step(weight, gradient, first_old, second, step_rate, decay_rate):
    first_new = BETA_FIRST * first_old + (1.0 - BETA_FIRST) * gradient
    second_new = BETA_SECOND * second + (1.0 - BETA_SECOND) * gradient * gradient
    first_hat = first_new / (1.0 - BETA_FIRST**STEP)
    second_hat = second_new / (1.0 - BETA_SECOND**STEP)
    updated = weight - step_rate * (
        first_hat / (jnp.sqrt(second_hat) + ADAM_EPS) + decay_rate * weight
    )
    return (second_new, updated)


def attend_row(qkv_row, seg_row):
    seq_len = seg_row.shape[0]
    blocked = min(512, seq_len)
    factor = qkv_row.shape[-1] ** (-0.5)
    key_rows = qkv_row[:, 1]
    value_rows = qkv_row[:, 2]
    outputs = []
    log_sums = []
    for offset in range(0, seq_len, blocked):
        queries = qkv_row[offset : offset + blocked, 0]
        seg_query = seg_row[offset : offset + blocked]
        scores = (
            jnp.einsum("qhe,khe->hqk", queries, key_rows, preferred_element_type=jnp.float32)
            * factor
        )
        matches = seg_query[:, None] == seg_row[None, :]
        scores = jnp.where(matches[None], scores, -1e30)
        row_peak = jnp.max(scores, axis=-1, keepdims=True)
        row_exp = jnp.exp(scores - row_peak)
        row_total = jnp.sum(row_exp, axis=-1, keepdims=True)
        soft_low = (row_exp / row_total).astype(jnp.bfloat16)
        mixed_block = jnp.einsum(
            "hqk,khe->qhe", soft_low, value_rows, preferred_element_type=jnp.float32
        )
        outputs.append(mixed_block.astype(jnp.bfloat16))
        log_sums.append((row_peak + jnp.log(row_total))[..., 0])
    return (jnp.concatenate(outputs, axis=0), jnp.concatenate(log_sums, axis=1))


def attend_back(qkv_row, seg_row, lse_row, grad_row):
    seq_len = seg_row.shape[0]
    blocked = min(512, seq_len)
    factor = qkv_row.shape[-1] ** (-0.5)
    key_rows = qkv_row[:, 1]
    value_rows = qkv_row[:, 2]
    grad_keys = jnp.zeros(key_rows.shape, jnp.float32)
    grad_values = jnp.zeros(value_rows.shape, jnp.float32)
    grad_query_list = []
    for offset in range(0, seq_len, blocked):
        queries = qkv_row[offset : offset + blocked, 0]
        seg_query = seg_row[offset : offset + blocked]
        scores = (
            jnp.einsum("qhe,khe->hqk", queries, key_rows, preferred_element_type=jnp.float32)
            * factor
        )
        matches = seg_query[:, None] == seg_row[None, :]
        shifted = jnp.where(
            matches[None], scores - lse_row[:, offset : offset + blocked, None], -1e30
        )
        weights = jnp.exp(shifted)
        weights_low = weights.astype(jnp.bfloat16)
        grad_out = grad_row[offset : offset + blocked]
        grad_values = grad_values + jnp.einsum(
            "hqk,qhe->khe", weights_low, grad_out, preferred_element_type=jnp.float32
        )
        grad_probs = jnp.einsum(
            "qhe,khe->hqk", grad_out, value_rows, preferred_element_type=jnp.float32
        )
        grad_scores = weights * (grad_probs - jnp.sum(grad_probs * weights, axis=-1, keepdims=True))
        scores_low = grad_scores.astype(jnp.bfloat16)
        grad_query_list.append(
            jnp.einsum("hqk,khe->qhe", scores_low, key_rows, preferred_element_type=jnp.float32)
            * factor
        )
        grad_keys = (
            grad_keys
            + jnp.einsum("hqk,qhe->khe", scores_low, queries, preferred_element_type=jnp.float32)
            * factor
        )
    return jnp.stack([jnp.concatenate(grad_query_list, axis=0), grad_keys, grad_values], axis=1)


def per_device(
    stream_in,
    dual_in,
    segment_ids,
    qkv_weight,
    proj_weight,
    up_weight,
    down_weight,
    vectors,
    qkv_first,
    proj_first,
    up_first,
    down_first,
    vec_first,
    qkv_second,
    proj_second,
    up_second,
    down_second,
    vec_second,
    cot_stream,
    cot_dual,
):
    rows_here = segment_ids.shape[0]
    seq_len = segment_ids.shape[1]
    model_width = stream_in.shape[1]
    head_count = model_width // HEAD
    qkv_full, proj_full, vec_full = (
        lax.all_gather(qkv_weight.astype(jnp.bfloat16), ("dp", "fsdp"), axis=0, tiled=True),
        lax.all_gather(proj_weight.astype(jnp.bfloat16), ("dp", "fsdp"), axis=0, tiled=True),
        lax.all_gather(vectors.astype(jnp.bfloat16), ("dp", "fsdp"), axis=0, tiled=True),
    )
    vec_all = vec_full.astype(jnp.float32)
    gain_one = vec_all[0:model_width]
    shift_one = vec_all[model_width : 2 * model_width]
    gain_two = vec_all[2 * model_width : 3 * model_width]
    shift_two = vec_all[3 * model_width : 4 * model_width]
    bias_q = vec_all[4 * model_width : 5 * model_width]
    bias_v = vec_all[5 * model_width : 6 * model_width]
    bias_o = vec_all[6 * model_width : 7 * model_width]
    bias_d = vec_all[7 * model_width : 8 * model_width]
    bias_u = vec_all[8 * model_width :]
    qkv_bias = jnp.concatenate([bias_q, jnp.zeros((model_width,), jnp.float32), bias_v])
    qkv_lin = jnp.dot(stream_in, qkv_full, preferred_element_type=jnp.float32) + qkv_bias
    qkv_low = qkv_lin.astype(jnp.bfloat16).reshape(rows_here, seq_len, 3, head_count, HEAD)
    mixed_rows, lse_rows = lax.map(
        lambda pieces: attend_row(pieces[0], pieces[1]), (qkv_low, segment_ids)
    )
    mixed_low = mixed_rows.reshape(-1, model_width)
    attn_out = jnp.dot(mixed_low, proj_full, preferred_element_type=jnp.float32) + bias_o
    first_sum = stream_in.astype(jnp.float32) + attn_out
    first_norm = normalize(first_sum, gain_one, shift_one)
    first_low = first_norm.astype(jnp.bfloat16)
    up_full, down_full = (
        lax.all_gather(up_weight.astype(jnp.bfloat16), ("dp", "fsdp"), axis=0, tiled=True),
        lax.all_gather(down_weight.astype(jnp.bfloat16), ("dp", "fsdp"), axis=0, tiled=True),
    )
    upper_lin = jnp.dot(first_low, up_full, preferred_element_type=jnp.float32) + bias_u
    hidden_low = smooth(upper_lin).astype(jnp.bfloat16)
    ffn_out = jnp.dot(hidden_low, down_full, preferred_element_type=jnp.float32) + bias_d
    second_sum = first_norm + ffn_out
    second_norm = normalize(second_sum, gain_two, shift_two)
    dual_out = dual_in + attn_out + ffn_out
    valid_mask = (segment_ids.reshape(-1, 1) != 0).astype(jnp.float32)
    local_sums = jnp.stack(
        [
            jnp.sum(valid_mask) * model_width,
            jnp.sum(valid_mask * second_norm * second_norm),
            jnp.sum(valid_mask * attn_out * attn_out),
            jnp.sum(valid_mask * ffn_out * ffn_out),
        ]
    )
    totals = lax.psum(local_sums, ("dp", "fsdp"))
    root_means = jnp.sqrt(totals[1:] / totals[0])
    cot_dual_f = cot_dual.astype(jnp.float32)
    _, norm_two_back = jax.vjp(normalize, second_sum, gain_two, shift_two)
    grad_two, grad_gain_two, grad_shift_two = norm_two_back(cot_stream.astype(jnp.float32))
    grad_ffn_low = (grad_two + cot_dual_f).astype(jnp.bfloat16)
    up_back, down_back = (
        lax.all_gather(up_weight.astype(jnp.bfloat16), ("dp", "fsdp"), axis=0, tiled=True),
        lax.all_gather(down_weight.astype(jnp.bfloat16), ("dp", "fsdp"), axis=0, tiled=True),
    )
    grad_down = jnp.einsum(
        "nf,nd->fd", hidden_low, grad_ffn_low, preferred_element_type=jnp.float32
    )
    grad_hidden = jnp.einsum(
        "nd,fd->nf", grad_ffn_low, down_back, preferred_element_type=jnp.float32
    )
    _, smooth_back = jax.vjp(smooth, upper_lin)
    (grad_upper,) = smooth_back(grad_hidden)
    grad_upper_low = grad_upper.astype(jnp.bfloat16)
    grad_up = jnp.einsum("nd,nf->df", first_low, grad_upper_low, preferred_element_type=jnp.float32)
    grad_first = (
        jnp.einsum("nf,df->nd", grad_upper_low, up_back, preferred_element_type=jnp.float32)
        + grad_two
    )
    up_grad, down_grad = (
        lax.psum_scatter(grad_up, ("dp", "fsdp"), scatter_dimension=0, tiled=True),
        lax.psum_scatter(grad_down, ("dp", "fsdp"), scatter_dimension=0, tiled=True),
    )
    _, norm_one_back = jax.vjp(normalize, first_sum, gain_one, shift_one)
    grad_one, grad_gain_one, grad_shift_one = norm_one_back(grad_first)
    grad_attn_low = (grad_one + cot_dual_f).astype(jnp.bfloat16)
    qkv_back, proj_back = (
        lax.all_gather(qkv_weight.astype(jnp.bfloat16), ("dp", "fsdp"), axis=0, tiled=True),
        lax.all_gather(proj_weight.astype(jnp.bfloat16), ("dp", "fsdp"), axis=0, tiled=True),
    )
    grad_proj = jnp.einsum(
        "nd,ne->de", mixed_low, grad_attn_low, preferred_element_type=jnp.float32
    )
    grad_mixed_low = jnp.einsum(
        "ne,de->nd", grad_attn_low, proj_back, preferred_element_type=jnp.float32
    ).astype(jnp.bfloat16)
    grad_rows = grad_mixed_low.reshape(rows_here, seq_len, head_count, HEAD)
    grad_qkv_rows = lax.map(
        lambda pieces: attend_back(pieces[0], pieces[1], pieces[2], pieces[3]),
        (qkv_low, segment_ids, lse_rows, grad_rows),
    )
    grad_qkv_low = grad_qkv_rows.reshape(-1, 3 * model_width).astype(jnp.bfloat16)
    grad_qkv = jnp.einsum("nd,ne->de", stream_in, grad_qkv_low, preferred_element_type=jnp.float32)
    stream_grad = (
        jnp.einsum("ne,de->nd", grad_qkv_low, qkv_back, preferred_element_type=jnp.float32)
        + grad_one
    )
    column_sums = jnp.sum(grad_qkv_low.astype(jnp.float32), axis=0)
    vec_local = jnp.concatenate(
        [
            grad_gain_one,
            grad_shift_one,
            grad_gain_two,
            grad_shift_two,
            column_sums[0:model_width],
            column_sums[2 * model_width :],
            jnp.sum(grad_attn_low.astype(jnp.float32), axis=0),
            jnp.sum(grad_ffn_low.astype(jnp.float32), axis=0),
            jnp.sum(grad_upper_low.astype(jnp.float32), axis=0),
        ]
    )
    qkv_grad, proj_grad, vec_grad = (
        lax.psum_scatter(grad_qkv, ("dp", "fsdp"), scatter_dimension=0, tiled=True),
        lax.psum_scatter(grad_proj, ("dp", "fsdp"), scatter_dimension=0, tiled=True),
        lax.psum_scatter(vec_local, ("dp", "fsdp"), scatter_dimension=0, tiled=True),
    )
    qkv_renewed, qkv_updated = adam_step(qkv_weight, qkv_grad, qkv_first, qkv_second, 0.04, 0.1)
    proj_renewed, proj_updated = adam_step(
        proj_weight, proj_grad, proj_first, proj_second, 0.15, 0.1
    )
    up_renewed, up_updated = adam_step(up_weight, up_grad, up_first, up_second, 0.04, 0.1)
    down_renewed, down_updated = adam_step(
        down_weight, down_grad, down_first, down_second, 0.03, 0.1
    )
    vec_renewed, vec_updated = adam_step(vectors, vec_grad, vec_first, vec_second, 0.2, 0.0)
    return (
        second_norm.astype(jnp.bfloat16),
        dual_out,
        stream_grad,
        root_means,
        qkv_grad,
        proj_grad,
        up_grad,
        down_grad,
        vec_grad,
        qkv_renewed,
        proj_renewed,
        up_renewed,
        down_renewed,
        vec_renewed,
        qkv_updated,
        proj_updated,
        up_updated,
        down_updated,
        vec_updated,
    )


def solution(mesh):
    in_specs = (
        P(("dp", "fsdp"), None),
        P(("dp", "fsdp"), None),
        P(("dp", "fsdp"), None),
        P(("dp", "fsdp"), None),
        P(("dp", "fsdp"), None),
        P(("dp", "fsdp"), None),
        P(("dp", "fsdp"), None),
        P(("dp", "fsdp")),
        P(("dp", "fsdp"), None),
        P(("dp", "fsdp"), None),
        P(("dp", "fsdp"), None),
        P(("dp", "fsdp"), None),
        P(("dp", "fsdp")),
        P(("dp", "fsdp"), None),
        P(("dp", "fsdp"), None),
        P(("dp", "fsdp"), None),
        P(("dp", "fsdp"), None),
        P(("dp", "fsdp")),
        P(("dp", "fsdp"), None),
        P(("dp", "fsdp"), None),
    )
    out_specs = (
        P(("dp", "fsdp"), None),
        P(("dp", "fsdp"), None),
        P(("dp", "fsdp"), None),
        P(),
        P(("dp", "fsdp"), None),
        P(("dp", "fsdp"), None),
        P(("dp", "fsdp"), None),
        P(("dp", "fsdp"), None),
        P(("dp", "fsdp")),
        P(("dp", "fsdp"), None),
        P(("dp", "fsdp"), None),
        P(("dp", "fsdp"), None),
        P(("dp", "fsdp"), None),
        P(("dp", "fsdp")),
        P(("dp", "fsdp"), None),
        P(("dp", "fsdp"), None),
        P(("dp", "fsdp"), None),
        P(("dp", "fsdp"), None),
        P(("dp", "fsdp")),
    )
    return jax.shard_map(
        per_device, mesh=mesh, in_specs=in_specs, out_specs=out_specs, check_vma=False
    )
```

profile of v0, /device:TPU:0, one launch (start us, length us, event | category | flops | bytes accessed | tf_op | source)
XLA Modules:
  0.0 931.9 jit_solution(15679125213624667584)
XLA Ops:
  13.1 42.2 %all-reduce = bf16[6144]{0:T(1024)(128)(2,1)S(1)} all-reduce(bf16[6144]{0:T(1024)(128)(2,1)S(1)} %dynamic-update-slice), channel_id=1, replica_groups=mesh['dp'=4,'fsdp'=8] {'dp','fsdp'}, use_global_device_ids=true, to_apply=%add | all-reduce | flops 6144 | bytes 24576
  58.6 45.2 %all_gather.21 = bf16[512,512]{1,0:T(8,128)(2,1)} all-gather(bf16[16,512]{1,0:T(8,128)(2,1)S(1)} %convert_element_type.124), channel_id=1, replica_groups=mesh['dp'=4,'fsdp'=8] {'dp','fsdp'}, dimensions={0}, use_global_device_ids=true | all-gather | bytes 540672 | tf_op jit(solution)/shard_map/all_gather | solution.py:138
  126.4 16.3 %reshape.289 = bf16[2,1024,3,8,64]{4,3,2,1,0:T(8,128)(2,1)} reshape(bf16[2048,1536]{1,0:T(8,128)(2,1)} %add_convert_fusion) | data formatting | bytes 12582912 | tf_op jit(solution)/shard_map/reshape | solution.py:153
  142.7 14.2 %copy.115 = bf16[2,1024,3,8,64]{1,4,3,2,0:T(8,128)(2,1)} copy(bf16[2,1024,3,8,64]{4,3,2,1,0:T(8,128)(2,1)} %reshape.289) | data formatting | bytes 12582912 | tf_op jit(solution)/shard_map/while | solution.py:154
  156.9 76.6 %while.22 = (s32[]{:T(128)}, bf16[2,1024,8,64]{1,3,2,0:T(8,128)(2,1)S(1)}, f32[2,8,1024]{2,1,0:T(8,128)S(1)}, bf16[2,1024,3,8,64]{1,4,3,2,0:T(8,128)(2,1)}, s32[...) while((s32[]{:T(128)}, bf16[2,1024,8,64]{1,3,2,0:T(8,128)(2,1)S(1)}, f32[2,8,1024]{2,1,0:T(8,128)S(1)}, ...), condition=%wide.region_5.6_spmd, body=%wide.region_0.5_spmd.sunk | while | flops 2251816960 | bytes 119890040 | solution.py:154
  170.7 11.0 %fusion.150 = (f32[8,512]{1,0:T(8,128)S(1)}, f32[8,512]{1,0:T(8,128)S(1)}) fusion(f32[8,512,1024]{2,1,0:T(8,128)} %get-tuple-element.386, f32[8,512]{1,0:T(8,128)S(1)} %get-tuple-element.387, pred[512,1024]{1,0:T(8,128)(4,1)S(1)} %get-tuple-element.385, f32[8,512]{1,0:T(8,128)S(1)} %get-tuple-element.388, f32[8,512,1024]{2,1,0:T(8,128)S(1)} %get-tuple-element.384, ...), kind=kLoop, calls=%fused_computation.8.clone.1 | loop fusion | flops 33546240 | bytes 34668544 | tf_op jit(solution)/shard_map/while/body/eval_jaxpr/reduce_sum | solution.py:57
  209.0 10.8 %fusion.150 = (f32[8,512]{1,0:T(8,128)S(1)}, f32[8,512]{1,0:T(8,128)S(1)}) fusion(f32[8,512,1024]{2,1,0:T(8,128)} %get-tuple-element.386, f32[8,512]{1,0:T(8,128)S(1)} %get-tuple-element.387, pred[512,1024]{1,0:T(8,128)(4,1)S(1)} %get-tuple-element.385, f32[8,512]{1,0:T(8,128)S(1)} %get-tuple-element.388, f32[8,512,1024]{2,1,0:T(8,128)S(1)} %get-tuple-element.384, ...), kind=kLoop, calls=%fused_computation.8.clone.1 | loop fusion | flops 33546240 | bytes 34668544 | tf_op jit(solution)/shard_map/while/body/eval_jaxpr/reduce_sum | solution.py:57
  245.7 16.5 %multiply_convert_fusion.2 = (bf16[2048,2048]{1,0:T(8,128)(2,1)}, f32[2048,2048]{1,0:T(8,128)}) fusion(f32[2048]{0:T(1024)S(1)} %copy-done.46, bf16[512,2048]{1,0:T(8,128)(2,1)} %all-gather.6.cloned.1.call-done, f32[2048,512]{0,1:T(8,128)} %copy-done.1, f32[512]{0:T(512)S(1)} %copy-done.50, f32[512]{0:T(512)S(1)} %copy-done.47, f32[2048]{0:T(1024)S(1)} %fusion.76, ...), kind=kOutput, calls=%fused_computation.85 | convolution fusion | flops 4342153216 | bytes 31485952 | tf_op jit(solution)/shard_map/dot_general | solution.py:166
  262.3 13.1 %fusion.96 = (f32[2048]{0:T(1024)S(1)}, f32[2048,512]{0,1:T(8,128)S(1)}, f32[2048,512]{0,1:T(8,128)}) fusion(f32[512]{0:T(512)S(1)} %copy-done.41, f32[512]{0:T(512)S(1)} %copy-done.50, f32[512]{0:T(512)S(1)} %copy-done.47, f32[2048]{0:T(1024)S(1)} %fusion.76, f32[2048,512]{0,1:T(8,128)} %copy-done.1, f32[2048]{0:T(1024)S(1)} %broadcast_multiply_fusion.1, ...), kind=kOutput, calls=%fused_computation.192 | convolution fusion | flops 4302305280 | bytes 23099392 | tf_op jit(solution)/shard_map/dot_general | solution.py:168
  290.6 22.4 %convert_reduce_fusion = (f32[2048]{0:T(1024)}, bf16[2048,2048]{1,0:T(8,128)(2,1)}) fusion(f32[2048,2048]{1,0:T(8,128)} %get-tuple-element.294, f32[2048]{0:T(1024)S(1)} %copy-done.46, bf16[2048,512]{0,1:T(8,128)(2,1)} %get-tuple-element.249, bf16[2048,512]{1,0:T(8,128)(2,1)} %all-gather.8.cloned.1.call-done), kind=kOutput, calls=%fused_computation.84 | convolution fusion | flops 4391434240 | bytes 29376512 | tf_op jit(solution)/shard_map/nd,fd->nf/dot_general | solution.py:194
  313.0 11.9 %multiply_reduce_fusion.2 = (f32[512]{0:T(512)}, f32[2048]{0:T(1024)S(1)}, f32[512]{0:T(512)}, f32[2048,512]{0,1:T(8,128)S(1)}) fusion(f32[2048,512]{0,1:T(8,128)S(1)} %copy-done.2, f32[2048]{0:T(1024)S(1)} %fusion.76, f32[2048]{0:T(1024)S(1)} %broadcast_multiply_fusion.1, f32[512]{0:T(512)S(1)} %copy-done.47, f32[2048]{0:T(1024)S(1)} %negate_multiply_fusion.1, ...), kind=kOutput, calls=%fused_computation.109 | convolution fusion | flops 4312790016 | bytes 25231360 | tf_op jit(solution)/shard_map/nf,df->nd/dot_general | solution.py:202
  343.9 169.9 %while.23 = (s32[]{:T(128)}, bf16[2,1024,3,8,64]{1,4,3,2,0:T(8,128)(2,1)}, bf16[2,1024,3,8,64]{1,4,3,2,0:T(8,128)(2,1)}, s32[2,1024]{1,0:T(2,128)S(1)}, f32[2,8,...) while((s32[]{:T(128)}, ...), condition=%wide.region_17.18_spmd, body=%wide.region_14.17_spmd.sunk | while | flops 5460451328 | bytes 401858784 | solution.py:223
  383.4 11.4 %multiply_convert_fusion.6 = bf16[8,512,1024]{2,1,0:T(8,128)(2,1)S(1)} fusion(f32[8,512,1024]{2,1,0:T(8,128)} %select_exponential_fusion.4, f32[8,512,1024]{2,1,0:T(8,128)} %get-tuple-element.405, f32[8,512]{1,0:T(8,128)S(1)} %get-tuple-element.406), kind=kLoop, calls=%fused_computation.37.clone.1 | loop fusion | flops 12582912 | bytes 41959424 | tf_op jit(solution)/shard_map/while/body/eval_jaxpr/convert_element_type | solution.py:97
  397.4 10.7 %multiply_reduce_fusion.8 = (f32[8,512]{1,0:T(8,128)S(1)}, f32[8,512,1024]{2,1,0:T(8,128)}) fusion(f32[8,512,1024]{2,1,0:T(8,128)} %copy-done, bf16[1024,3,8,64]{0,3,2,1:T(8,128)(2,1)S(1)} %dynamic-slice_bitcast_fusion.18, bf16[2,1024,8,64]{1,3,2,0:T(8,128)(2,1)} %get-tuple-element.454, s32[]{:T(128)S(6)} %copy.160), kind=kOutput, calls=%fused_computation.41.clone.1 | convolution fusion | flops 545255424 | bytes 35143684 | tf_op jit(solution)/shard_map/while/body/eval_jaxpr/qhe,khe->hqk/dot_general | solution.py:93
  408.2 11.4 %multiply_convert_fusion.5 = bf16[8,512,1024]{2,1,0:T(8,128)(2,1)S(1)} fusion(f32[8,512,1024]{2,1,0:T(8,128)} %copy-done, f32[8,512,1024]{2,1,0:T(8,128)} %get-tuple-element.403, f32[8,512]{1,0:T(8,128)S(1)} %get-tuple-element.404), kind=kLoop, calls=%fused_computation.40.clone.1 | loop fusion | flops 12582912 | bytes 41959424 | tf_op jit(solution)/shard_map/while/body/eval_jaxpr/convert_element_type | solution.py:97
  457.4 10.8 %multiply_reduce_fusion.9 = (f32[8,512]{1,0:T(8,128)S(1)}, f32[8,512,1024]{2,1,0:T(8,128)}) fusion(f32[8,512,1024]{2,1,0:T(8,128)} %select_exponential_fusion.4, bf16[1024,3,8,64]{0,3,2,1:T(8,128)(2,1)S(1)} %dynamic-slice_bitcast_fusion.18, bf16[2,1024,8,64]{1,3,2,0:T(8,128)(2,1)} %get-tuple-element.454, s32[]{:T(128)S(6)} %copy.160, s32[]{:T(128)S(6)} %add.482), kind=kOutput, calls=%fused_computation.38.clone.1 | convolution fusion | flops 545255424 | bytes 35143688 | tf_op jit(solution)/shard_map/while/body/eval_jaxpr/qhe,khe->hqk/dot_general | solution.py:93
  468.2 11.3 %multiply_convert_fusion.6 = bf16[8,512,1024]{2,1,0:T(8,128)(2,1)S(1)} fusion(f32[8,512,1024]{2,1,0:T(8,128)} %select_exponential_fusion.4, f32[8,512,1024]{2,1,0:T(8,128)} %get-tuple-element.405, f32[8,512]{1,0:T(8,128)S(1)} %get-tuple-element.406), kind=kLoop, calls=%fused_computation.37.clone.1 | loop fusion | flops 12582912 | bytes 41959424 | tf_op jit(solution)/shard_map/while/body/eval_jaxpr/convert_element_type | solution.py:97
  482.1 10.7 %multiply_reduce_fusion.8 = (f32[8,512]{1,0:T(8,128)S(1)}, f32[8,512,1024]{2,1,0:T(8,128)}) fusion(f32[8,512,1024]{2,1,0:T(8,128)} %copy-done, bf16[1024,3,8,64]{0,3,2,1:T(8,128)(2,1)S(1)} %dynamic-slice_bitcast_fusion.18, bf16[2,1024,8,64]{1,3,2,0:T(8,128)(2,1)} %get-tuple-element.454, s32[]{:T(128)S(6)} %copy.160), kind=kOutput, calls=%fused_computation.41.clone.1 | convolution fusion | flops 545255424 | bytes 35143684 | tf_op jit(solution)/shard_map/while/body/eval_jaxpr/qhe,khe->hqk/dot_general | solution.py:93
  492.9 11.3 %multiply_convert_fusion.5 = bf16[8,512,1024]{2,1,0:T(8,128)(2,1)S(1)} fusion(f32[8,512,1024]{2,1,0:T(8,128)} %copy-done, f32[8,512,1024]{2,1,0:T(8,128)} %get-tuple-element.403, f32[8,512]{1,0:T(8,128)S(1)} %get-tuple-element.404), kind=kLoop, calls=%fused_computation.40.clone.1 | loop fusion | flops 12582912 | bytes 41959424 | tf_op jit(solution)/shard_map/while/body/eval_jaxpr/convert_element_type | solution.py:97
  513.8 11.9 %copy.124 = bf16[2,1024,3,8,64]{1,0,4,3,2:T(2,128)(2,1)S(1)} copy(bf16[2,1024,3,8,64]{1,4,3,2,0:T(8,128)(2,1)} %get-tuple-element.81) | data formatting | bytes 12582912 | tf_op jit(solution)/shard_map/convert_element_type | solution.py:227
  548.4 11.4 %fusion.83 = f32[512,2048]{1,0:T(8,128)} fusion(bf16[2048,2048]{1,0:T(8,128)(2,1)} %get-tuple-element.298, f32[2048,512]{0,1:T(8,128)} %copy-done.1, f32[512]{0:T(512)S(1)} %copy-done.51, f32[512]{0:T(512)S(1)} %copy-done.48, f32[2048]{0:T(1024)S(1)} %copy-done.39, f32[2048]{0:T(1024)S(1)} %copy-done.30), kind=kOutput, calls=%fused_computation.188 | convolution fusion | flops 4300210176 | bytes 16797696 | tf_op jit(solution)/shard_map/nd,nf->df/dot_general | solution.py:200
  567.4 37.9 %all-reduce.2 = (f32[4]{0:T(128)S(1)}, f32[6144]{0:T(1024)S(1)}) all-reduce(f32[4]{0:T(128)S(1)} %pad_maximum_fusion.1, f32[6144]{0:T(1024)S(1)} %constant_dynamic-update-slice_fusion), channel_id=1, replica_groups=mesh['dp'=4,'fsdp'=8] {'dp','fsdp'}, use_global_device_ids=true, to_apply=%region_22.23 | all-reduce | flops 6148 | bytes 49184 | tf_op jit(solution)/shard_map/psum | solution.py:181
  637.8 142.9 %reduce-scatter.11.cloned.1.call-done = f32[64,512]{1,0:T(8,128)} async-done(((f32[2048,512]{1,0:T(8,128)}), f32[64,512]{1,0:T(8,128)}) %reduce-scatter.11.cloned.1.call-update) | async-done | bytes 131088 | tf_op jit(solution)/shard_map/reduce_scatter | solution.py:207
  782.4 140.7 %reduce-scatter.9.cloned.1.call-done = f32[16,2048]{1,0:T(8,128)} async-done(((f32[512,2048]{1,0:T(8,128)}), f32[16,2048]{1,0:T(8,128)}) %reduce-scatter.9.cloned.1.call-update) | async-done | bytes 131088 | tf_op jit(solution)/shard_map/reduce_scatter | solution.py:206
  (275 shorter events, 288.8 us)
Async XLA Ops:
  7.2 100.5 %copy-start.12 = (bf16[2048,512]{1,0:T(8,128)(2,1)S(1)}, bf16[2048,512]{1,0:T(8,128)(2,1)}, u32[]{:S(2)}) copy-start(bf16[2048,512]{1,0:T(8,128)(2,1)} %param.43) | copy-start | bytes 6291460
  7.2 112.5 %all-gather.4.cloned.1.call-start = ((), (), s32[]{:S(2)}) async-start(), calls=%async_computation.4 | async-start | bytes 1622016 | tf_op jit(solution)/shard_map/all_gather | solution.py:137
  8.9 236.7 %all-gather.6.cloned.1.call-start = ((), (), s32[]{:S(2)}) async-start(), calls=%async_computation.5 | async-start | bytes 2162688 | tf_op jit(solution)/shard_map/all_gather | solution.py:163
  10.5 251.7 %all-gather.8.cloned.1.call-start = ((), (), s32[]{:S(2)}) async-start(), calls=%async_computation.6 | async-start | bytes 2162688 | tf_op jit(solution)/shard_map/all_gather | solution.py:164
  12.2 617.9 %reduce-scatter.7.cloned.1.call-start = ((), (), s32[]{:S(2)}) async-start(), calls=%async_computation.7 | async-start | bytes 1081344 | tf_op jit(solution)/shard_map/reduce_scatter | solution.py:249
  142.7 14.2 %copy-start.15 = (bf16[2,1024,8,64]{1,3,2,0:T(8,128)(2,1)S(1)}, bf16[2,1024,8,64]{1,3,2,0:T(8,128)(2,1)}, u32[]{:S(2)}) copy-start(bf16[2,1024,8,64]{1,3,2,0:T(8,128)(2,1)} %custom-call.1) | copy-start | bytes 6291460
  142.7 14.2 %copy-start.18 = (s32[2,1024]{1,0:T(2,128)S(1)}, s32[2,1024]{1,0:T(2,128)}, u32[]{:S(2)}) copy-start(s32[2,1024]{1,0:T(2,128)} %param.26) | copy-start | bytes 24580
  243.1 81.8 %copy-start.29 = (f32[2048]{0:T(1024)}, f32[2048]{0:T(1024)S(1)}, u32[]{:S(2)}) copy-start(f32[2048]{0:T(1024)S(1)} %broadcast_multiply_fusion.1) | copy-start | bytes 24580
  245.6 79.3 %copy-start.38 = (f32[2048]{0:T(1024)}, f32[2048]{0:T(1024)S(1)}, u32[]{:S(2)}) copy-start(f32[2048]{0:T(1024)S(1)} %fusion.76) | copy-start | bytes 24580
  245.7 16.6 %copy-start.41 = (f32[512]{0:T(512)S(1)}, f32[512]{0:T(512)}, u32[]{:S(2)}) copy-start(f32[512]{0:T(512)} %get-tuple-element.284) | copy-start | bytes 6148
  290.6 22.4 %copy-start.2 = (f32[2048,512]{0,1:T(8,128)S(1)}, f32[2048,512]{0,1:T(8,128)}, u32[]{:S(2)}) copy-start(f32[2048,512]{0,1:T(8,128)} %copy-done.1) | copy-start | bytes 12582916
  334.7 301.4 %reduce-scatter.13.cloned.1.call-start = ((), (), s32[]{:S(2)}) async-start(), calls=%async_computation.10 | async-start | bytes 3244032
  351.7 18.3 %copy-start = (f32[8,512,1024]{2,1,0:T(8,128)}, f32[8,512,1024]{2,1,0:T(8,128)S(1)}, u32[]{:S(2)}) copy-start(f32[8,512,1024]{2,1,0:T(8,128)S(1)} %select_exponential_fusion.5) | copy-start | bytes 50331652 | tf_op jit(solution)/shard_map/while
  436.3 18.4 %copy-start = (f32[8,512,1024]{2,1,0:T(8,128)}, f32[8,512,1024]{2,1,0:T(8,128)S(1)}, u32[]{:S(2)}) copy-start(f32[8,512,1024]{2,1,0:T(8,128)S(1)} %select_exponential_fusion.5) | copy-start | bytes 50331652 | tf_op jit(solution)/shard_map/while
  537.0 243.7 %reduce-scatter.11.cloned.1.call-start = ((), (), s32[]{:S(2)}) async-start(), calls=%async_computation.9 | async-start | bytes 4325376 | tf_op jit(solution)/shard_map/reduce_scatter | solution.py:207
  547.7 375.4 %reduce-scatter.9.cloned.1.call-start = ((), (), s32[]{:S(2)}) async-start(), calls=%async_computation.8 | async-start | bytes 4325376 | tf_op jit(solution)/shard_map/reduce_scatter | solution.py:206
  559.9 45.4 %copy-start.9 = (bf16[2048,512]{0,1:T(8,128)(2,1)S(1)}, bf16[2048,512]{0,1:T(8,128)(2,1)}, u32[]{:S(2)}) copy-start(bf16[2048,512]{0,1:T(8,128)(2,1)} %get-tuple-element.279) | copy-start | bytes 6291460
  561.2 46.6 %copy-start.37 = (f32[2048]{0:T(1024)S(1)}, f32[2048]{0:T(1024)}, u32[]{:S(2)}) copy-start(f32[2048]{0:T(1024)} %copy-done.36) | copy-start | bytes 24580
  623.1 157.5 %copy-start.19 = (f32[64,512]{1,0:T(8,128)S(1)}, f32[64,512]{1,0:T(8,128)}, u32[]{:S(2)}) copy-start(f32[64,512]{1,0:T(8,128)} %param.30) | copy-start | bytes 393220
  623.2 157.5 %copy-start.23 = (f32[64,512]{1,0:T(8,128)S(1)}, f32[64,512]{1,0:T(8,128)}, u32[]{:S(2)}) copy-start(f32[64,512]{1,0:T(8,128)} %param.35) | copy-start | bytes 393220
  623.2 157.5 %copy-start.24 = (f32[64,512]{1,0:T(8,128)S(1)}, f32[64,512]{1,0:T(8,128)}, u32[]{:S(2)}) copy-start(f32[64,512]{1,0:T(8,128)} %param.40) | copy-start | bytes 393220
  623.2 299.9 %copy-start.20 = (f32[16,2048]{1,0:T(8,128)S(1)}, f32[16,2048]{1,0:T(8,128)}, u32[]{:S(2)}) copy-start(f32[16,2048]{1,0:T(8,128)} %param.29) | copy-start | bytes 393220
  623.2 299.9 %copy-start.25 = (f32[16,2048]{1,0:T(8,128)S(1)}, f32[16,2048]{1,0:T(8,128)}, u32[]{:S(2)}) copy-start(f32[16,2048]{1,0:T(8,128)} %param.34) | copy-start | bytes 393220
  623.2 299.9 %copy-start.26 = (f32[16,2048]{1,0:T(8,128)S(1)}, f32[16,2048]{1,0:T(8,128)}, u32[]{:S(2)}) copy-start(f32[16,2048]{1,0:T(8,128)} %param.39) | copy-start | bytes 393220
  (46 other events, 235.8 us)
Sparse Core Ops, SparseCore 0:
  11.6 57.8 all-gather.3
  73.0 55.5 all-gather.5
  132.2 55.3 all-gather.7
  334.8 132.4 reduce-scatter.6
  537.1 99.0 reduce-scatter.12
  639.0 141.6 reduce-scatter.10
  783.6 139.4 reduce-scatter.8
where the time goes:
time: 938 us; the launch traced here: 932 us
  waiting for transfers between devices  288 us (31%)
  matrix products  274 us (29%)
  blocking collectives  125 us (13%)
  local copies, waits for them, and re-layouts  116 us (12%)
  other arithmetic  111 us (12%)
  between operations  15.7 us (2%)
    reduce_scatter x1, waiting for transfers between devices, per_device(): lax.psum_scatter(grad_down, ('dp', 'fsdp'), scatter_dimension=0, tiled=True)  143 us
    reduce_scatter x1, waiting for transfers between devices, per_device(): lax.psum_scatter(grad_up, ('dp', 'fsdp'), scatter_dimension=0, tiled=True)  141 us
    convert_element_type x4, other arithmetic, attend_back(): scores_low = grad_scores.astype(jnp.bfloat16)  45.4 us
    all_gather x1, blocking collectives, per_device(): lax.all_gather(proj_weight.astype(jnp.bfloat16), ('dp', 'fsdp'), axis=0,...  45.2 us
    unnamed x131, local copies, waits for them, and re-layouts  44.2 us
    dot_general x4, matrix products, attend_back(): jnp.einsum('qhe,khe->hqk', grad_out, value_rows, preferred_element_type=j...  42.9 us
    unnamed x1, blocking collectives  42.2 us
    psum x1, blocking collectives, per_device(): totals = lax.psum(local_sums, ('dp', 'fsdp'))  37.9 us
  transfers between devices with their start and end apart: 7, of which 3 were waited for; matrix products, arithmetic and copies ran while one was open for 44% of the time, Pallas kernels for 0%

commit v1 on v0

v1 whole, which is shorter than its diff:
```python
import functools

import jax
import jax.numpy as jnp
from jax import lax
from jax.experimental import pallas as pl
from jax.experimental.pallas import tpu as pltpu
from jax.sharding import PartitionSpec as P

HEAD = 64
STEP = 10
NORM_EPS = 1e-05
BETA_FIRST = 0.5
BETA_SECOND = 0.5
ADAM_EPS = 1e-08
RATES = ((0.04, 0.1), (0.15, 0.1), (0.04, 0.1), (0.03, 0.1), (0.2, 0.0))

AXES = ("dp", "fsdp")
MESH = pl.DeviceIdType.MESH
bf16 = jnp.bfloat16
f32 = jnp.float32
ANY = pl.BlockSpec(memory_space=pl.ANY)
VMEM = pl.BlockSpec(memory_space=pltpu.VMEM)

SLOTS = 32
NEG = -1e30
QB = 256
LANES = 128


def nn(a, b):
    return jnp.dot(a, b, preferred_element_type=f32)


def nt(a, b):
    return lax.dot_general(a, b, (((1,), (1,)), ((), ())), preferred_element_type=f32)


def tn(a, b):
    return lax.dot_general(a, b, (((0,), (0,)), ((), ())), preferred_element_type=f32)


def merged(packed):
    return packed.reshape(-1, packed.shape[-1])


def half_rows():
    lane = lax.broadcasted_iota(jnp.int32, (1, LANES), 1)
    low = jnp.where(lane < HEAD, 1.0, 0.0)
    return low.astype(bf16), (1.0 - low).astype(bf16)


def segment_columns(seg_row):
    length = seg_row.shape[-1]
    place = lax.rem(lax.broadcasted_iota(jnp.int32, (LANES, length), 0), HEAD)
    ids = jnp.broadcast_to(seg_row, (LANES, length))
    same = (place == ids) & (place < 16)
    ones = jnp.where(same, 1.0, 0.0)
    against = jnp.where(place < 16, jnp.where(same, 0.0, NEG), jnp.where(place < 19, 1.0, 0.0))
    return jnp.transpose(ones).astype(bf16), jnp.transpose(against).astype(bf16)


def in_parts(value):
    first = value.astype(bf16).astype(f32)
    rest = value - first
    second = rest.astype(bf16).astype(f32)
    return first, second, rest - second


def part_columns(value, other):
    first, second, third = in_parts(value)
    lane = lax.rem(lax.broadcasted_iota(jnp.int32, value.shape, 1), HEAD)
    return jnp.where(
        lane == 16, first, jnp.where(lane == 17, second, jnp.where(lane == 18, third, other))
    )


class Place:
    def __init__(self):
        self.dp = lax.axis_index("dp")
        self.fs = lax.axis_index("fsdp")
        self.c = lax.rem(self.fs, 2)
        self.z = self.fs // 2
        x = lax.rem(self.dp, 2)
        y = self.dp // 2
        self.dpx = 2 * y + 1 - x
        self.dpy = 2 - 2 * y + x
        self.a = self.dpx + self.c * (self.dpy - self.dpx)
        self.b = self.dpy + self.c * (self.dpx - self.dpy)
        self.ab = 3 - self.dp
        self.zs = [lax.rem(self.z + k, 4) for k in range(4)]
        self.to_a = (self.a, self.fs)
        self.to_b = (self.b, self.fs)
        self.to_x = (self.dpx, self.fs)
        self.to_y = (self.dpy, self.fs)
        self.to_core = (self.dp, self.fs + 1 - 2 * self.c)
        self.to_z = [None] + [(self.dp, 2 * self.zs[k] + self.c) for k in range(1, 4)]

    def greet(self):
        barrier = pltpu.get_barrier_semaphore()
        friends = [self.to_a, self.to_b, self.to_core] + self.to_z[1:]
        for friend in friends:
            pl.semaphore_signal(barrier, inc=1, device_id=friend, device_id_type=MESH)
        pl.semaphore_wait(barrier, len(friends))


def remote(src, dst, send_sem, recv_sem, device):
    return pltpu.make_async_remote_copy(
        src_ref=src,
        dst_ref=dst,
        send_sem=send_sem,
        recv_sem=recv_sem,
        device_id=device,
        device_id_type=MESH,
    )


class Gather:
    def __init__(self, here, buf, send_sem, recv_sem):
        self.here, self.buf, self.send_sem, self.recv_sem = here, buf, send_sem, recv_sem
        self.sent = []

    def copy(self, number, d, z, c, device):
        slot = self.buf.at[d, z, c]
        return remote(slot, slot, self.send_sem.at[number], self.recv_sem.at[d, z, c], device)

    def send(self, d, z, device):
        number = len(self.sent)
        self.sent.append((number, d, z, device))
        self.copy(number, d, z, self.here.c, device).start()

    def arrive(self, d, z, c):
        self.copy(0, d, z, c, self.here.to_core).wait_recv()

    def step(self, number):
        me = self.here
        if number == 0:
            for k in range(1, 4):
                self.send(me.dp, me.z, me.to_z[k])
            for device in (me.to_a, me.to_b, me.to_core):
                self.send(me.dp, me.z, device)
        elif number < 4:
            self.arrive(me.dp, me.zs[number], me.c)
            for device in (me.to_b, me.to_a, me.to_core):
                self.send(me.dp, me.zs[number], device)
        elif number < 8:
            self.arrive(me.a, me.zs[number - 4], me.c)
            self.send(me.a, me.zs[number - 4], me.to_b)
            self.send(me.a, me.zs[number - 4], me.to_core)
        elif number < 12:
            self.arrive(me.b, me.zs[number - 8], me.c)
            self.send(me.b, me.zs[number - 8], me.to_core)
        elif number < 16:
            self.arrive(me.ab, me.zs[number - 12], me.c)
            self.send(me.ab, me.zs[number - 12], me.to_core)
        else:
            for d in range(4):
                for z in range(4):
                    self.arrive(d, z, 1 - me.c)

    def finish(self):
        for number, d, z, device in self.sent:
            self.copy(number, d, z, self.here.c, device).wait_send()


def forward_kernel(comm, scale, *refs):
    if comm:
        (x_hbm, seg, wqkv, wp, wu, wd, vec, qkv_o, mix_o, feat_o, vec_o, ga_o, gb_o, gc_o) = refs[:14]
        (x_v, qkv_v, mix_v, feat_v, fq, fk, ga, gb, gc) = refs[14:23]
        (loc, sa, ra, sb, rb, sc, rc) = refs[23:]
    else:
        (x_hbm, seg, ga_hbm, qkv_o, mix_o, feat_o, vec_o) = refs[:7]
        (x_v, qkv_v, mix_v, feat_v, fq, fk, ga) = refs[7:14]
        (loc,) = refs[14:]
    rows, length = seg.shape
    width = x_v.shape[1]
    pairs = width // LANES
    step_rows = width // SLOTS

    x_copy = pltpu.make_async_copy(x_hbm, x_v, loc.at[0])
    if comm:
        here = Place()
        here.greet()
        x_copy.start()
        own = (here.dp, here.z, here.c)
        for j in range(3):
            ga[own + (slice(j * step_rows, (j + 1) * step_rows),)] = wqkv[
                :, j * width : (j + 1) * width
            ].astype(bf16)
        index = here.dp * 8 + here.fs
        count = vec.shape[1]
        begin = index * count
        top = begin // width
        shift = begin - top * width
        line = jnp.concatenate([vec[...], jnp.zeros((1, width - count), f32)], axis=1)
        line = pltpu.roll(jnp.broadcast_to(line, (8, width)), shift, 1)
        line = jnp.concatenate([line, line], axis=0)
        row = lax.broadcasted_iota(jnp.int32, (16, width), 0)
        lane = lax.broadcasted_iota(jnp.int32, (16, width), 1)
        kept = ((row == top) & (lane >= shift)) | ((row == top + 1) & (lane < shift))
        ga[own + (slice(48, 64),)] = jnp.where(kept, line, 0.0).astype(bf16)
        first = Gather(here, ga, sa, ra)
        first.step(0)
        gb[own + (slice(0, step_rows),)] = wp[...].astype(bf16)
        for j in range(4):
            gb[own + (slice((j + 1) * step_rows, (j + 2) * step_rows),)] = wu[
                :, j * width : (j + 1) * width
            ].astype(bf16)
        gc[own] = wd[...].astype(bf16)
    else:
        x_copy.start()
        ga_copy = pltpu.make_async_copy(ga_hbm, ga, loc.at[1])
        ga_copy.start()

    for r in range(rows):
        ones, against = segment_columns(seg[r : r + 1, :])
        fq[r] = ones
        fk[r] = against

    if comm:
        for number in range(1, 17):
            first.step(number)
        second = Gather(here, gb, sb, rb)
        third = Gather(here, gc, sc, rc)
        second.step(0)
        third.step(0)
    else:
        ga_copy.wait()
    x_copy.wait()

    vec_sum = jnp.sum(ga[:, :, :, 48:64, :].astype(f32).reshape(SLOTS, 16, width), axis=0)
    vec_o[...] = vec_sum

    def project(t, carry):
        span = pl.ds(pl.multiple_of(t * 512, 512), 512)
        tile = x_v[span, :]
        for j in range(3):
            lin = nn(tile, merged(ga[:, :, :, j * step_rows : (j + 1) * step_rows, :]))
            if j == 0:
                lin = (lin + vec_sum[4:5]).astype(bf16).astype(f32) * scale
            if j == 2:
                lin = lin + vec_sum[5:6]
            low = lin.astype(bf16)
            for p in range(pairs):
                qkv_v[pairs * j + p, span, :] = low[:, p * LANES : (p + 1) * LANES]
        return carry

    lax.fori_loop(0, x_v.shape[0] // 512, project, 0)
    qkv_copy = pltpu.make_async_copy(qkv_v, qkv_o, loc.at[2])
    qkv_copy.start()
    low_half, high_half = half_rows()
    half = lax.broadcasted_iota(jnp.int32, (QB, LANES), 1) < HEAD

    def out_copies(r):
        span = pl.ds(pl.multiple_of(r * length, length), length)
        return (
            pltpu.make_async_copy(mix_v.at[span, :], mix_o.at[span, :], loc.at[3 + 2 * r]),
            pltpu.make_async_copy(feat_v.at[span, :], feat_o.at[span, :], loc.at[4 + 2 * r]),
        )

    def attend(i, carry):
        r = i // pairs
        p = lax.rem(i, pairs)
        span = pl.ds(pl.multiple_of(r * length, length), length)
        keys = qkv_v[pairs + p, span, :]
        values = qkv_v[2 * pairs + p, span, :]
        keys_in = (keys * low_half + fk[r] * high_half, keys * high_half + fk[r] * low_half)
        one_low = jnp.broadcast_to(low_half, values.shape)
        one_high = jnp.broadcast_to(high_half, values.shape)
        values_in = (
            jnp.concatenate([values * low_half, one_low], axis=1),
            jnp.concatenate([values * high_half, one_high], axis=1),
        )

        def scores(j, h):
            part = pl.ds(pl.multiple_of(r * length + j * QB, QB), QB)
            query = qkv_v[p, part, :]
            marks = fq[r, j * QB : (j + 1) * QB, :]
            mine, other = (low_half, high_half) if h == 0 else (high_half, low_half)
            return nt(query * mine + marks * other, keys_in[h])

        blocks = [(j, h) for j in range(length // QB) for h in range(2)]
        following = scores(*blocks[0])
        kept = []
        for number, (j, h) in enumerate(blocks):
            current = following
            if number + 1 < len(blocks):
                following = scores(*blocks[number + 1])
            peak = jnp.max(current, axis=1, keepdims=True)
            soft = jnp.exp(current - peak).astype(bf16)
            kept.append((peak, nn(soft, values_in[h])))
            if h == 1:
                both = kept[0][1] + kept[1][1]
                total = both[:, LANES:]
                part = pl.ds(pl.multiple_of(r * length + j * QB, QB), QB)
                columns = pl.ds(pl.multiple_of(p * LANES, LANES), LANES)
                mix_v[part, columns] = (both[:, :LANES] / total).astype(bf16)
                logs = jnp.where(half, kept[0][0], kept[1][0]) + jnp.log(total)
                logs = pltpu.roll(logs, HEAD, 1)
                marks = fq[r, j * QB : (j + 1) * QB, :].astype(f32)
                feat_v[part, columns] = part_columns(-logs, marks).astype(bf16)
                kept = []
        if comm:
            for number in range(16):
                pl.when(i == number // 2)(functools.partial(second.step, number + 1))
                pl.when(i == number // 2)(functools.partial(third.step, number + 1))
        for r_done in range(rows):

            @pl.when(i == (r_done + 1) * pairs - 1)
            def _():
                for copy in out_copies(r_done):
                    copy.start()

        return carry

    lax.fori_loop(0, rows * pairs, attend, 0)
    if comm:
        first.finish()
        second.finish()
        third.finish()
        copies = [
            pltpu.make_async_copy(src, dst, loc.at[3 + 2 * rows + k])
            for k, (src, dst) in enumerate(((ga, ga_o), (gb, gb_o), (gc, gc_o)))
        ]
        for copy in copies:
            copy.start()
        for copy in copies:
            copy.wait()
    qkv_copy.wait()
    for r in range(rows):
        for copy in out_copies(r):
            copy.wait()


def row_mean(value):
    return jnp.mean(value, axis=-1, keepdims=True)


def column_sum(value):
    return jnp.sum(value, axis=0, keepdims=True)


def middle_kernel(
    seg, vec, x_hbm, mix_hbm, dual_hbm, cs_hbm, cd_hbm, gb_hbm, gc_hbm,
    so_o, do_o, one_o, gm_o, pg_o, vg_o,
    x_v, mix_v, dual_v, cs_v, cd_v, gb, gc, low_v, spread_v, two_v, ffn_v, hid_v, slope_v, up_v, pg_v,
    in_sem, out_sem, w_sem,
):
    rows, length = seg.shape
    tokens, width = x_v.shape
    blocks = hid_v.shape[0]
    step_rows = width // SLOTS
    tile = 256
    tiles = tokens // tile
    per_row = length // tile

    def rows_of(t, size=tile):
        return pl.ds(pl.multiple_of(t * size, size), size)

    w_copies = [
        pltpu.make_async_copy(gb_hbm, gb, w_sem.at[0]),
        pltpu.make_async_copy(gc_hbm, gc, w_sem.at[1]),
    ]
    pairs_in = ((mix_hbm, mix_v), (x_hbm, x_v), (cs_hbm, cs_v), (cd_hbm, cd_v), (dual_hbm, dual_v))

    def in_copy(k, t):
        src, dst = pairs_in[k]
        return pltpu.make_async_copy(src.at[rows_of(t)], dst.at[rows_of(t)], in_sem.at[k, t])

    w_copies[0].start()
    for k in range(5):
        in_copy(k, 0).start()
    w_copies[1].start()
    for t in range(1, tiles):
        for k in range(5):
            in_copy(k, t).start()
    pairs_out = ((cs_v, so_o), (dual_v, do_o), (two_v, one_o), (ffn_v, gm_o))

    def out_copy(k, t):
        src, dst = pairs_out[k]
        return pltpu.make_async_copy(src.at[rows_of(t)], dst.at[rows_of(t)], out_sem.at[k, t])

    vg_o[...] = jnp.zeros_like(vg_o)
    gain_one, shift_one, gain_two, shift_two = (vec[k : k + 1, :] for k in range(4))
    bias_o, bias_d = vec[6:7, :], vec[7:8, :]
    w_copies[0].wait()
    w_copies[1].wait()
    lane = lax.broadcasted_iota(jnp.int32, (1, width), 1)

    def proj_weight():
        return merged(gb[:, :, :, 0:step_rows, :])

    def up_weight(f):
        return merged(gb[:, :, :, (f + 1) * step_rows : (f + 2) * step_rows, :])

    def down_weight(f):
        return merged(gc[f])

    def forward(t, carry):
        here = rows_of(t)
        for k in range(5):
            in_copy(k, t).wait()
        attn = nn(mix_v[here, :], proj_weight()) + bias_o
        first_sum = x_v[here, :].astype(f32) + attn
        centred = first_sum - row_mean(first_sum)
        spread = lax.rsqrt(row_mean(centred * centred) + NORM_EPS)
        hat = centred * spread
        x_v[here, :] = hat.astype(bf16)
        spread_v[here, :] = jnp.broadcast_to(spread, (tile, LANES))
        first_norm = hat * gain_one + shift_one
        first_low = first_norm.astype(bf16)
        low_v[here, :] = first_low
        ffn = bias_d
        for f in range(blocks):
            u = nn(first_low, up_weight(f)) + vec[8 + f : 9 + f, :]
            square = u * u
            inner = jnp.tanh(u * (0.7978845608028654 + 0.035677408136300125 * square))
            share = 0.5 + 0.5 * inner
            hidden = (u * share).astype(bf16)
            slope = share + 0.5 * u * (1.0 - inner * inner) * (
                0.7978845608028654 + 0.10703222440890037 * square
            )
            hid_v[f, here, :] = hidden
            slope_v[f, here, :] = slope.astype(bf16)
            ffn = ffn + nn(hidden, down_weight(f))
        dual_v[here, :] = dual_v[here, :] + attn + ffn
        second_sum = first_norm + ffn
        centred = second_sum - row_mean(second_sum)
        spread = lax.rsqrt(row_mean(centred * centred) + NORM_EPS)
        hat = centred * spread
        second_norm = hat * gain_two + shift_two
        cot = cs_v[here, :].astype(f32)
        cs_v[here, :] = second_norm.astype(bf16)
        out_copy(0, t).start()
        out_copy(1, t).start()
        r = t // per_row
        ids = seg[pl.ds(r, 1), pl.ds(pl.multiple_of((t - r * per_row) * tile, tile), tile)]
        valid = jnp.where(ids != 0, 1.0, 0.0)
        valid = jnp.transpose(jnp.broadcast_to(valid, (LANES, tile)))[:, 0:1]
        counts = column_sum(valid) * width
        squares = [
            jnp.sum(column_sum(valid * v * v), axis=1, keepdims=True)
            for v in (second_norm, attn, ffn)
        ]
        line = jnp.where(lane == 0, counts, 0.0)
        for k in range(3):
            line = jnp.where(lane == k + 1, squares[k], line)
        vg_o[12:13, :] += line
        scaled = cot * gain_two
        grad = (scaled - row_mean(scaled) - hat * row_mean(scaled * hat)) * spread
        two_v[here, :] = grad
        vg_o[2:3, :] += column_sum(cot * hat)
        vg_o[3:4, :] += column_sum(cot)
        grad_low = (grad + cd_v[here, :].astype(f32)).astype(bf16)
        ffn_v[here, :] = grad_low
        vg_o[7:8, :] += column_sum(grad_low.astype(f32))
        return carry

    lax.fori_loop(0, tiles, forward, 0)

    for f in range(blocks):

        def back(t, carry, f=f):
            here = rows_of(t, 512)
            grad = nt(ffn_v[here, :], down_weight(f))
            grad_up = (slope_v[f, here, :].astype(f32) * grad).astype(bf16)
            up_v[here, :] = grad_up
            vg_o[8 + f : 9 + f, :] += column_sum(grad_up.astype(f32))
            two_v[here, :] += nt(grad_up, up_weight(f))
            return carry

        lax.fori_loop(0, tokens // 512, back, 0)
        down = tn(hid_v[f], ffn_v[...])
        pg_v[f, :, :, 5 * step_rows :, :] = down.astype(bf16).reshape(4, 2, 4 * step_rows, width)
        up = tn(low_v[...], up_v[...])
        pg_v[:, :, :, (f + 1) * step_rows : (f + 2) * step_rows, :] = up.astype(bf16).reshape(
            4, 4, 2, step_rows, width
        )

    def back_first(t, carry):
        here = rows_of(t)
        grad = two_v[here, :]
        hat = x_v[here, :].astype(f32)
        vg_o[0:1, :] += column_sum(grad * hat)
        vg_o[1:2, :] += column_sum(grad)
        scaled = grad * gain_one
        spread = spread_v[here, 0:1]
        grad_one = (scaled - row_mean(scaled) - hat * row_mean(scaled * hat)) * spread
        two_v[here, :] = grad_one
        out_copy(2, t).start()
        grad_low = (grad_one + cd_v[here, :].astype(f32)).astype(bf16)
        low_v[here, :] = grad_low
        vg_o[6:7, :] += column_sum(grad_low.astype(f32))
        ffn_v[here, :] = nt(grad_low, proj_weight()).astype(bf16)
        out_copy(3, t).start()
        return carry

    lax.fori_loop(0, tiles, back_first, 0)
    proj = tn(mix_v[...], low_v[...])
    pg_v[:, :, :, 0:step_rows, :] = proj.astype(bf16).reshape(4, 4, 2, step_rows, width)
    pg_copy = pltpu.make_async_copy(pg_v, pg_o, w_sem.at[2])
    pg_copy.start()
    for t in range(tiles):
        for k in range(4):
            out_copy(k, t).wait()
    pg_copy.wait()


class Scatter:
    def __init__(self, here, send, mine, bufs, send_sem, recv_sem):
        self.here, self.source, self.mine = here, send, mine
        self.from_core, self.from_b, self.from_a, self.from_z = bufs
        self.send_sem, self.recv_sem = send_sem, recv_sem

    def copies(self, phase):
        me, mine = self.here, self.mine
        if phase == 0:
            found = [(self.source, self.from_core, me.to_core)]
        elif phase == 1:
            found = [
                (mine.at[me.b], self.from_b.at[0], me.to_b),
                (mine.at[me.ab], self.from_b.at[1], me.to_b),
            ]
        elif phase == 2:
            found = [(mine.at[me.a], self.from_a, me.to_a)]
        else:
            found = [
                (mine.at[me.dp, me.zs[k]], self.from_z.at[k - 1], me.to_z[k]) for k in range(1, 4)
            ]
        base = (0, 1, 3, 4)[phase]
        return [
            remote(src, dst, self.send_sem.at[base + k], self.recv_sem.at[base + k], device)
            for k, (src, dst, device) in enumerate(found)
        ]

    def start(self, phase):
        for copy in self.copies(phase):
            copy.start()

    def add(self, phase):
        me, mine = self.here, self.mine
        for copy in self.copies(phase):
            copy.wait_recv()

        def into(where, part):
            mine[where] = (mine[where].astype(f32) + part.astype(f32)).astype(bf16)

        if phase == 0:
            for d in range(4):
                for z in range(4):
                    into((d, z), self.from_core[d, z])
        elif phase == 1:
            for z in range(4):
                into((me.dp, z), self.from_b[0, z])
                into((me.a, z), self.from_b[1, z])
        elif phase == 2:
            for z in range(4):
                into((me.dp, z), self.from_a[z])

    def result(self):
        for copy in self.copies(3):
            copy.wait_recv()
        total = self.mine[self.here.dp, self.here.z].astype(f32)
        for k in range(3):
            total = total + self.from_z[k].astype(f32)
        return total

    def finish(self):
        for phase in range(4):
            for copy in self.copies(phase):
                copy.wait_send()


class Total:
    def __init__(self, here, parts, bufs, send_sem, recv_sem):
        self.here, self.parts, self.bufs = here, parts, bufs
        self.send_sem, self.recv_sem = send_sem, recv_sem

    def copies(self, phase):
        me, parts, bufs = self.here, self.parts, self.bufs
        if phase < 3:
            device = (me.to_core, me.to_y, me.to_x)[phase]
            found = [(parts.at[phase], bufs.at[phase], device)]
        else:
            found = [(bufs.at[3 + me.z], bufs.at[3 + me.z], me.to_z[k]) for k in range(1, 4)]
        made = []
        for k, (src, dst, device) in enumerate(found):
            recv = self.recv_sem.at[phase] if phase < 3 else self.recv_sem.at[3 + me.z]
            made.append(remote(src, dst, self.send_sem.at[phase + k], recv, device))
        return made

    def start(self, phase):
        for copy in self.copies(phase):
            copy.start()

    def add(self, phase):
        for copy in self.copies(phase):
            copy.wait_recv()
        total = self.parts[phase] + self.bufs[phase]
        if phase < 2:
            self.parts[phase + 1] = total
        else:
            self.bufs[3 + self.here.z] = total

    def result(self):
        me = self.here
        for k in range(1, 4):
            slot = self.bufs.at[3 + me.zs[k]]
            remote(slot, slot, self.send_sem.at[0], self.recv_sem.at[3 + me.zs[k]], me.to_core).wait_recv()
        return self.bufs[3] + self.bufs[4] + self.bufs[5] + self.bufs[6]

    def finish(self):
        for phase in range(4):
            for copy in self.copies(phase):
                copy.wait_send()


def backward_kernel(comm, scale, *refs):
    (seg, vg, qkv_hbm, feat_hbm, mix_hbm, gm_hbm, one_hbm, x_hbm, ga_hbm) = refs[:9]
    if comm:
        (pg_hbm, sg_o, tot_o, totq_o, vg_o) = refs[9:14]
        refs = refs[14:]
    else:
        (sg_o, pq_o, vg_o) = refs[9:12]
        refs = refs[12:]
    (qkv_v, feat_v, mix_v, gm_v, one_v, x_v, ga, gq_v, fk, pq_v, in_sem, w_sem, out_sem) = refs[:13]
    rows, length = seg.shape
    tokens, width = x_v.shape
    pairs = width // LANES
    step_rows = width // SLOTS

    def pair_copies(p):
        columns = pl.ds(pl.multiple_of(p * LANES, LANES), LANES)
        found = [(qkv_hbm.at[j * pairs + p], qkv_v.at[j * pairs + p]) for j in range(3)]
        found += [
            (src.at[:, columns], dst.at[:, columns])
            for src, dst in ((gm_hbm, gm_v), (mix_hbm, mix_v), (feat_hbm, feat_v))
        ]
        return [
            pltpu.make_async_copy(src, dst, in_sem.at[p, k]) for k, (src, dst) in enumerate(found)
        ]

    late = [
        pltpu.make_async_copy(src, dst, w_sem.at[k])
        for k, (src, dst) in enumerate(((x_hbm, x_v), (ga_hbm, ga), (one_hbm, one_v)))
    ]
    if comm:
        (mine, fc, fb, fa, fz, mine_q, qc, qb, qa, qz, vp, vb, s1, r1, s2, r2, s3, r3) = refs[13:]
        here = Place()
        here.greet()
        weights = Scatter(here, pg_hbm.at[:, :, 1 - here.c], mine, (fc, fb, fa, fz), s1, r1)
        columns_of = [
            Scatter(
                here,
                pq_v.at[p, :, :, 1 - here.c],
                mine_q.at[p],
                (qc.at[p], qb.at[p], qa.at[p], qz.at[p]),
                s2.at[p],
                r2.at[p],
            )
            for p in range(pairs)
        ]
        sums = Total(here, vp, vb, s3, r3)
        mine_copy = pltpu.make_async_copy(pg_hbm.at[:, :, here.c], mine, w_sem.at[3])
    for copy in pair_copies(0):
        copy.start()
    if comm:
        weights.start(0)
        mine_copy.start()
    for p in range(1, pairs):
        for copy in pair_copies(p):
            copy.start()
    for copy in late:
        copy.start()
    for r in range(rows):
        fk[r] = segment_columns(seg[r : r + 1, :])[1]
    low_half, high_half = half_rows()

    def attend(i, carry):
        p = i // rows
        r = lax.rem(i, rows)
        span = pl.ds(pl.multiple_of(r * length, length), length)
        columns = pl.ds(pl.multiple_of(p * LANES, LANES), LANES)

        @pl.when(r == 0)
        def _():
            for copy in pair_copies(p):
                copy.wait()

        queries = qkv_v[p, span, :]
        keys = qkv_v[pairs + p, span, :]
        values = qkv_v[2 * pairs + p, span, :]
        grads = gm_v[span, columns]
        marks = feat_v[span, columns]
        product = grads.astype(f32) * mix_v[span, columns].astype(f32)
        is_low = lax.broadcasted_iota(jnp.int32, product.shape, 1) < HEAD
        for_low = jnp.sum(jnp.where(is_low, product, 0.0), axis=1, keepdims=True)
        for_high = jnp.sum(jnp.where(is_low, 0.0, product), axis=1, keepdims=True)
        deltas = part_columns(-jnp.where(is_low, for_high, for_low), 0.0).astype(bf16)
        place = lax.rem(lax.broadcasted_iota(jnp.int32, (1, LANES), 1), HEAD)
        ones = jnp.where((place >= 16) & (place < 19), 1.0, 0.0).astype(bf16)
        queries_t = jnp.transpose(queries)
        grads_t = jnp.transpose(grads)
        key_parts, value_parts = [], []
        query_grads = [None] * (length // QB)
        for h in range(2):
            mine_h, other_h = (low_half, high_half) if h == 0 else (high_half, low_half)
            half = slice(h * HEAD, (h + 1) * HEAD)
            key_own = keys * mine_h
            key_in = key_own + fk[r] * other_h
            value_in = values * mine_h + ones * other_h
            key_sum = value_sum = None
            for j in range(length // QB):
                part = slice(j * QB, (j + 1) * QB)
                soft = jnp.exp(nt(queries[part] * mine_h + marks[part] * other_h, key_in))
                wide = nt(grads[part] * mine_h + deltas[part] * other_h, value_in)
                back = (soft * wide).astype(bf16)
                soft = soft.astype(bf16)
                moved = nn(back, key_own)
                query_grads[j] = moved if h == 0 else query_grads[j] + moved
                value_part = nn(grads_t[half, part], soft)
                key_part = nn(queries_t[half, part], back)
                value_sum = value_part if j == 0 else value_sum + value_part
                key_sum = key_part if j == 0 else key_sum + key_part
            key_parts.append(key_sum)
            value_parts.append(value_sum)
        for j in range(length // QB):
            part = pl.ds(pl.multiple_of(r * length + j * QB, QB), QB)
            gq_v[0, part, columns] = (query_grads[j] * scale).astype(bf16)
        gq_v[1, span, columns] = jnp.transpose(jnp.concatenate(key_parts, axis=0)).astype(bf16)
        gq_v[2, span, columns] = jnp.transpose(jnp.concatenate(value_parts, axis=0)).astype(bf16)

        @pl.when(r == rows - 1)
        def _():
            @pl.when(p == 0)
            def _():
                late[0].wait()

            stacked = jnp.concatenate([gq_v[j, :, columns] for j in range(3)], axis=1)
            grad = tn(x_v[...], stacked).astype(bf16).reshape(4, 4, 2, step_rows, 3 * LANES)
            for j in range(3):
                pq_v[p, :, :, :, j * step_rows : (j + 1) * step_rows, :] = grad[
                    ..., j * LANES : (j + 1) * LANES
                ]

        return carry

    lax.fori_loop(0, rows * pairs, attend, 0)
    late[1].wait()
    late[2].wait()

    vg_sum = vg[...]
    row = lax.broadcasted_iota(jnp.int32, vg_sum.shape, 0)
    for k, j in ((4, 0), (5, 2)):
        vg_sum = jnp.where(row == k, column_sum(gq_v[j].astype(f32)), vg_sum)

    if comm:
        vp[0] = vg_sum
        mine_copy.wait()
        for p in range(pairs):
            mine_q[p] = pq_v[p, :, :, here.c]
        groups = columns_of + [weights]
        for group in columns_of:
            group.start(0)
        sums.start(0)
        for phase in range(3):
            for group in groups:
                group.add(phase)
                group.start(phase + 1)
            sums.add(phase)
            sums.start(phase + 1)
    else:
        vg_o[...] = vg_sum
        pq_copy = pltpu.make_async_copy(pq_v, pq_o, out_sem.at[4])
        pq_copy.start()

    def out_copy(t):
        span = pl.ds(pl.multiple_of(t * 512, 512), 512)
        return pltpu.make_async_copy(one_v.at[span, :], sg_o.at[span, :], out_sem.at[t])

    def stream(t, carry):
        span = pl.ds(pl.multiple_of(t * 512, 512), 512)
        total = one_v[span, :]
        for j in range(3):
            total = total + nt(
                gq_v[j, span, :], merged(ga[:, :, :, j * step_rows : (j + 1) * step_rows, :])
            )
        one_v[span, :] = total
        out_copy(t).start()
        return carry

    lax.fori_loop(0, tokens // 512, stream, 0)
    if comm:
        tot_o[...] = weights.result()
        for p in range(pairs):
            totq_o[p] = columns_of[p].result()
        vg_o[...] = sums.result()
        for group in groups + [sums]:
            group.finish()
    else:
        pq_copy.wait()
    for t in range(tokens // 512):
        out_copy(t).wait()


def adam(weight, gradient, first_old, second, rates):
    step_rate, decay_rate = rates
    first_new = BETA_FIRST * first_old + (1.0 - BETA_FIRST) * gradient
    second_new = BETA_SECOND * second + (1.0 - BETA_SECOND) * gradient * gradient
    first_hat = first_new / (1.0 - BETA_FIRST**STEP)
    second_hat = second_new / (1.0 - BETA_SECOND**STEP)
    updated = weight - step_rate * (
        first_hat / (jnp.sqrt(second_hat) + ADAM_EPS) + decay_rate * weight
    )
    return second_new, updated


def update_kernel(tot, totq, vg, *refs):
    weights, firsts, seconds = refs[0:5], refs[5:10], refs[10:15]
    root, grads, renewed, updated = refs[15], refs[16:21], refs[21:26], refs[26:31]
    width = tot.shape[1]
    step_rows = width // SLOTS
    pairs = width // LANES

    def apply(k, columns, gradient):
        where = (slice(None), columns)
        grads[k][where] = gradient
        renewed[k][where], updated[k][where] = adam(
            weights[k][where], gradient, firsts[k][where], seconds[k][where], RATES[k]
        )

    for j in range(3):
        for p in range(pairs):
            begin = j * width + p * LANES
            apply(0, slice(begin, begin + LANES), totq[p, j * step_rows : (j + 1) * step_rows, :])
    apply(1, slice(None), tot[0:step_rows, :])
    for j in range(4):
        apply(2, slice(j * width, (j + 1) * width), tot[(j + 1) * step_rows : (j + 2) * step_rows, :])
    apply(3, slice(None), tot[5 * step_rows :, :])
    count = weights[4].shape[1]
    begin = (lax.axis_index("dp") * 8 + lax.axis_index("fsdp")) * count
    top = begin // width
    shift = begin - top * width
    row = lax.broadcasted_iota(jnp.int32, vg.shape, 0)
    lane = lax.broadcasted_iota(jnp.int32, vg.shape, 1)
    kept = ((row == top) & (lane >= shift)) | ((row == top + 1) & (lane < shift))
    line = column_sum(jnp.where(kept, vg[...], 0.0))
    line = pltpu.roll(jnp.broadcast_to(line, (8, width)), lax.rem(width - shift, width), 1)
    apply(4, slice(None), line[0:1, :count])
    sums = vg[12:13, 0:LANES]
    root[...] = jnp.sqrt(sums / sums[:, 0:1])


def params(**more):
    return pltpu.CompilerParams(vmem_limit_bytes=62 * 2**20, **more)


def shape(dims, kind):
    return jax.ShapeDtypeStruct(dims, kind)


def pack_columns(full, blocks):
    width = full.shape[0]
    parts = full.reshape(SLOTS, width // SLOTS, blocks, width)
    return jnp.swapaxes(parts, 1, 2).reshape(SLOTS, -1, width)


def unpack_columns(packed, blocks):
    width = packed.shape[-1]
    parts = packed.reshape(SLOTS, blocks, width // SLOTS, width)
    return jnp.swapaxes(parts, 1, 2).reshape(width, blocks * width)


def per_device(comm, *args):
    (stream_in, dual_in, segment_ids) = args[:3]
    weights, firsts, seconds = args[3:8], args[8:13], args[13:18]
    cot_stream, cot_dual = args[18:]
    tokens, width = stream_in.shape
    rows, length = segment_ids.shape
    pairs = width // LANES
    hidden = weights[2].shape[1]
    blocks = hidden // width
    unit = width // SLOTS
    scale = HEAD**-0.5
    slots = (4, 4, 2)
    dma = pltpu.SemaphoreType.DMA
    sem_gather = [dma((31,)), dma(slots)]
    rows_a, rows_b, rows_c = 4 * unit, 5 * unit, 4 * unit
    ga_shape, gb_shape, gc_shape = (slots + (n, width) for n in (rows_a, rows_b, rows_c))

    def vm(dims, kind=bf16):
        return pltpu.VMEM(dims, kind)

    flat = (tokens, width)
    common_out = [
        shape((3 * pairs, tokens, LANES), bf16),
        shape(flat, bf16),
        shape(flat, bf16),
        shape((16, width), f32),
    ]
    common_scratch = [
        vm(flat),
        vm((3 * pairs, tokens, LANES)),
        vm(flat),
        vm(flat),
        vm((rows, length, LANES)),
        vm((rows, length, LANES)),
        vm(ga_shape),
    ]
    cost = pl.CostEstimate(flops=8 * 10**9, bytes_accessed=2 * 10**7, transcendentals=2 * 10**7)
    if comm:
        masters = [w if w.ndim == 2 else w.reshape(1, -1) for w in weights]
        qkv, mix, feat, vec, ga, gb, gc = pl.pallas_call(
            functools.partial(forward_kernel, True, scale),
            out_shape=common_out + [shape(s, bf16) for s in (ga_shape, gb_shape, gc_shape)],
            in_specs=[ANY] + [VMEM] * 6,
            out_specs=[ANY] * 3 + [VMEM] + [ANY] * 3,
            scratch_shapes=common_scratch
            + [vm(gb_shape), vm(gc_shape), dma((16,))]
            + sem_gather * 3,
            compiler_params=params(collective_id=0, has_side_effects=True),
            cost_estimate=cost,
            name="gather_forward",
        )(stream_in, segment_ids, *masters)
    else:
        full = [lax.all_gather(w.astype(bf16), AXES, axis=0, tiled=True) for w in weights]
        vec_pad = jnp.pad(full[4].reshape(-1, width), ((0, 4), (0, 0)))
        vec_pad = jnp.concatenate([vec_pad[None], jnp.zeros((SLOTS - 1, 16, width), bf16)], axis=0)
        ga = jnp.concatenate([pack_columns(full[0], 3), vec_pad], axis=1).reshape(ga_shape)
        gb = jnp.concatenate(
            [pack_columns(full[1], 1), pack_columns(full[2], blocks)], axis=1
        ).reshape(gb_shape)
        gc = full[3].reshape(gc_shape)
        qkv, mix, feat, vec = pl.pallas_call(
            functools.partial(forward_kernel, False, scale),
            out_shape=common_out,
            in_specs=[ANY, VMEM, ANY],
            out_specs=[ANY] * 3 + [VMEM],
            scratch_shapes=common_scratch + [dma((16,))],
            compiler_params=params(),
            cost_estimate=cost,
            name="forward",
        )(stream_in, segment_ids, ga)

    pg_shape = slots + (9 * unit, width)
    tiles = tokens // 256
    stream_out, dual_out, grad_one, grad_mixed, pg, vg = pl.pallas_call(
        middle_kernel,
        out_shape=[
            shape(flat, bf16),
            shape(flat, f32),
            shape(flat, f32),
            shape(flat, bf16),
            shape(pg_shape, bf16),
            shape((16, width), f32),
        ],
        in_specs=[VMEM, VMEM] + [ANY] * 7,
        out_specs=[ANY] * 5 + [VMEM],
        scratch_shapes=[
            vm(flat),
            vm(flat),
            vm(flat, f32),
            vm(flat),
            vm(flat),
            vm(gb_shape),
            vm(gc_shape),
            vm(flat),
            vm((tokens, LANES), f32),
            vm(flat, f32),
            vm(flat),
            vm((blocks, tokens, width)),
            vm((blocks, tokens, width)),
            vm(flat),
            vm(pg_shape),
            dma((5, tiles)),
            dma((4, tiles)),
            dma((3,)),
        ],
        compiler_params=params(),
        cost_estimate=pl.CostEstimate(
            flops=3 * 10**10, bytes_accessed=4 * 10**7, transcendentals=4 * 10**6
        ),
        name="feed_forward",
    )(segment_ids, vec, stream_in, mix, dual_in, cot_stream, cot_dual, gb, gc)

    pq_shape = (pairs,) + slots + (3 * unit, LANES)
    scratch = [
        vm((3 * pairs, tokens, LANES)),
        vm(flat),
        vm(flat),
        vm(flat),
        vm(flat, f32),
        vm(flat),
        vm(ga_shape),
        vm((3,) + flat),
        vm((rows, length, LANES)),
        vm(pq_shape),
        dma((pairs, 6)),
        dma((4,)),
        dma((8,)),
    ]
    operands = (segment_ids, vg, qkv, feat, mix, grad_mixed, grad_one, stream_in, ga)
    cost = pl.CostEstimate(flops=2 * 10**10, bytes_accessed=3 * 10**7, transcendentals=2 * 10**7)
    if comm:
        tail = (9 * unit, width)
        tail_q = (3 * unit, LANES)
        stream_grad, tot, totq, vg = pl.pallas_call(
            functools.partial(backward_kernel, True, scale),
            out_shape=[
                shape(flat, f32),
                shape(tail, f32),
                shape((pairs,) + tail_q, f32),
                shape((16, width), f32),
            ],
            in_specs=[VMEM, VMEM] + [ANY] * 8,
            out_specs=[ANY] + [VMEM] * 3,
            scratch_shapes=scratch
            + [vm(s + tail) for s in ((4, 4), (4, 4), (2, 4), (4,), (3,))]
            + [vm((pairs,) + s + tail_q) for s in ((4, 4), (4, 4), (2, 4), (4,), (3,))]
            + [vm((3, 16, width), f32), vm((7, 16, width), f32)]
            + [dma((7,)), dma((7,)), dma((pairs, 7)), dma((pairs, 7)), dma((6,)), dma((7,))],
            compiler_params=params(collective_id=1, has_side_effects=True),
            cost_estimate=cost,
            name="backward_scatter",
        )(*operands, pg)
        outs = pl.pallas_call(
            update_kernel,
            out_shape=[shape((1, LANES), f32)]
            + [shape(w.shape, f32) for _ in range(3) for w in masters],
            in_specs=[VMEM] * 18,
            out_specs=[VMEM] * 16,
            compiler_params=params(),
            name="update",
        )(tot, totq, vg, *masters, *firsts[:4], firsts[4].reshape(1, -1), *seconds[:4], seconds[4].reshape(1, -1))
        root_means = outs[0][0, 1:4]
        grads, renewed, updated = (
            [v.reshape(w.shape) for v, w in zip(outs[k : k + 5], weights)] for k in (1, 6, 11)
        )
    else:
        stream_grad, pq, vg = pl.pallas_call(
            functools.partial(backward_kernel, False, scale),
            out_shape=[shape(flat, f32), shape(pq_shape, bf16), shape((16, width), f32)],
            in_specs=[VMEM, VMEM] + [ANY] * 7,
            out_specs=[ANY, ANY, VMEM],
            scratch_shapes=scratch,
            compiler_params=params(),
            cost_estimate=cost,
            name="backward",
        )(*operands)
        pq = jnp.moveaxis(pq.reshape(pairs, SLOTS, 3 * unit, LANES), 0, 2).reshape(SLOTS, 3 * unit, width)
        pg = pg.reshape(SLOTS, 9 * unit, width)
        partial = [
            unpack_columns(pq, 3),
            unpack_columns(pg[:, :unit], 1),
            unpack_columns(pg[:, unit : 5 * unit], blocks),
            pg[:, 5 * unit :].reshape(hidden, width),
            vg[:12].reshape(-1),
        ]
        grads = [
            lax.psum_scatter(g.astype(f32), AXES, scatter_dimension=0, tiled=True) for g in partial
        ]
        totals = lax.psum(vg[12, :4], AXES)
        root_means = jnp.sqrt(totals[1:] / totals[0])
        made = [adam(*four) for four in zip(weights, grads, firsts, seconds, RATES)]
        renewed, updated = ([m[k] for m in made] for k in range(2))
    return (stream_out, dual_out, stream_grad, root_means, *grads, *renewed, *updated)


def solution(mesh):
    sizes = dict(mesh.shape)
    comm = sizes["dp"] == 4 and sizes["fsdp"] == 8
    matrix, line = P(AXES, None), P(AXES)
    five = (matrix, matrix, matrix, matrix, line)
    in_specs = (matrix,) * 3 + five * 3 + (matrix, matrix)
    out_specs = (matrix,) * 3 + (P(),) + five * 3
    return jax.shard_map(
        functools.partial(per_device, comm),
        mesh=mesh,
        in_specs=in_specs,
        out_specs=out_specs,
        check_vma=False,
    )
```

time: 938 us -> 246 us (0.26)
  waiting for transfers between devices: 288 us -> 0 us
  matrix products: 274 us -> 0 us
  Pallas kernels: 0 us -> 239 us
  blocking collectives: 125 us -> 0 us
  other arithmetic: 111 us -> 0 us
  local copies, waits for them, and re-layouts: 116 us -> 5.88 us
  between operations: 15.7 us -> 0.68 us
    reduce_scatter x3 -> x0, waiting for transfers between devices: 284 us -> none  [the longest x1 143 us: per_device(): lax.psum_scatter(grad_down, ('dp', 'fsdp'), scatter_dimension=0, tiled=True)]
    dot_general x40 -> x0, matrix products: 274 us -> none  [the longest x4 42.9 us: attend_back(): jnp.einsum('qhe,khe->hqk', grad_out, value_rows, preferred_element_type=j...]
    pallas_call x0 -> x4, Pallas kernels: none -> 239 us  [the longest x1 105 us: per_device(): pl.pallas_call(functools.partial(backward_kernel, True, scale), out_shape...]
    convert_element_type x9 -> x0, other arithmetic: 51.6 us -> none  [the longest x4 45.4 us: attend_back(): scores_low = grad_scores.astype(jnp.bfloat16)]
    all_gather x1 -> x0, blocking collectives: 45.2 us -> none  [per_device(): lax.all_gather(proj_weight.astype(jnp.bfloat16), ('dp', 'fsdp'), axis=0,...]
    reduce_sum x10 -> x0, other arithmetic: 44.7 us -> none  [the longest x2 21.8 us: attend_row(): row_total = jnp.sum(row_exp, axis=-1, keepdims=True)]
    unnamed x1 -> x0, blocking collectives: 42.2 us -> none
    unnamed x131 -> x1, local copies, waits for them, and re-layouts: 44.2 us -> 4.64 us
  transfers between devices with their start and end apart: 7 -> 0, of which waited for: 3 -> 0; matrix products, arithmetic and copies ran while one was open for 44% -> 0% of each run, Pallas kernels for 0% -> 0%
where the time goes in v1:
time: 246 us
  Pallas kernels  239 us (97%)
  local copies, waits for them, and re-layouts  5.88 us (2%)
    pallas_call x1, Pallas kernels, per_device(): pl.pallas_call(functools.partial(backward_kernel, True, scale), out_shape...  105 us
    pallas_call x1, Pallas kernels, per_device(): pl.pallas_call(functools.partial(forward_kernel, True, scale), out_shape=...  67.2 us
    pallas_call x1, Pallas kernels, per_device(): pl.pallas_call(middle_kernel, out_shape=[shape(flat, bf16), shape(flat, f...  64.7 us

profile of v1, /device:TPU:0, one launch (start us, length us, event | category | flops | bytes accessed | tf_op | source)
XLA Modules:
  0.0 245.7 jit_solution(17535532017789207407)
XLA Ops:
  0.7 67.2 %gather_forward.1 = (bf16[12,2048,128]{2,1,0:T(8,128)(2,1)}, bf16[2048,512]{1,0:T(8,128)(2,1)}, bf16[2048,512]{1,0:T(8,128)(2,1)}, f32[16,512]{1,0:T(8,128)}, bf...) custom-call(bf16[2048,512]{1,0:T(8,128)(2,1)} %refs_7_.2, ...), custom_call_target="tpu_custom_call" | custom-call | flops 8000000000 | bytes 20000000 | tf_op jit(solution)/shard_map/gather_forward/pallas_call | solution.py:913
  67.9 64.7 %feed_forward.1 = (bf16[2048,512]{1,0:T(8,128)(2,1)}, f32[2048,512]{1,0:T(8,128)}, f32[2048,512]{1,0:T(8,128)}, bf16[2048,512]{1,0:T(8,128)(2,1)}, bf16[4,4,2,14...) custom-call(s32[2,1024]{1,0:T(2,128)} %refs_0_.4, f32[16,512]{1,0:T(8,128)} %get-tuple-element.52.vec, ...), custom_call_target="tpu_custom_call" | custom-call | flops 30000001024 | bytes 40000000 | tf_op jit(solution)/shard_map/feed_forward/pallas_call | solution.py:947
  132.6 104.6 %backward_scatter.1 = (f32[2048,512]{1,0:T(8,128)}, f32[144,512]{1,0:T(8,128)}, f32[4,48,128]{2,1,0:T(8,128)}, f32[16,512]{1,0:T(8,128)}) custom-call(s32[2,1024]{1,0:T(2,128)} %refs_0_.4, f32[16,512]{1,0:T(8,128)} %get-tuple-element.58.refs_1_, bf16[12,2048,128]{2,1,0:T(8,128)(2,1)} %get-tuple-element.59.refs_2_, ...), custom_call_target="tpu_custom_call" | custom-call | flops 20000000000 | bytes 30000000 | tf_op jit(solution)/shard_map/backward_scatter/pallas_call | solution.py:1007
  237.2 2.7 %update.1 = (f32[1,128]{1,0:T(1,128)}, f32[16,1536]{1,0:T(8,128)}, f32[16,512]{1,0:T(8,128)}, f32[16,2048]{1,0:T(8,128)}, f32[64,512]{1,0:T(8,128)}, /*index=5*/...) custom-call(f32[144,512]{1,0:T(8,128)} %get-tuple-element.66.tot, ...), custom_call_target="tpu_custom_call" | custom-call | tf_op jit(solution)/shard_map/update/pallas_call | solution.py:1026
  239.8 1.2 slice_bitcast_fusion
  241.1 4.6 %copy.40 = f32[2048,512]{1,0:T(8,128)} copy(f32[2048,512]{1,0:T(8,128)} %get-tuple-element.106) | data formatting | bytes 8388608
